TPU v7x, 256 devices: a whole 4x4x8 slice. The times are simulated.
256 devices in a mesh: enc: 16 (over x, y), blk: 16 (over z, core).
Axes of the slice: x: 4, y: 4, z: 8, core: 2. Of those that a mesh axis runs over, the one named last changes fastest.
Arguments:
- observations: bfloat16 [131072, 128], P(('enc', 'blk')), may hold values from -6 to 6
- lon_index: int32 [256, 512], P(('enc', 'blk')), may hold values from 0 to 1439
- live_count: int32 [256, 256], P(('enc', 'blk')), may hold values from 0 to 2, as said below
- w_in: bfloat16 [128, 512], replicated, may hold values from -0.5 to 0.5
- w_out: bfloat16 [512, 512], replicated, may hold values from -0.25 to 0.25
- w_spec: float32 [256, 512], replicated, may hold values from -4 to 4
- north: float32 [256, 512], P(('enc', 'blk')), may hold values from -0.8 to 0.8
- south: float32 [256, 512], P(('enc', 'blk')), may hold values from -0.8 to 0.8
- w_mix: bfloat16 [512, 512], replicated, may hold values from -0.25 to 0.25
- loss_sensitivity: bfloat16 [256, 1440, 512], P(('enc', 'blk')), may hold values from -6 to 6
Outputs:
- predicted_state: bfloat16 [256, 1440, 512], P(('enc', 'blk'))
- entry_matrix_slope: float32 [128, 512], replicated
- exit_matrix_slope: float32 [512, 512], replicated
- blend_matrix_slope: float32 [512, 512], replicated
- observation_slope: bfloat16 [131072, 128], P(('enc', 'blk'))
Inputs may be any that keep to these rules, and one draw needn't show every extreme that they name: In every draw some cycle r has live_count[r, s] = 2 for every source s.
All inputs are finite; a program needn't handle non-finite values.
Results may differ from a plain program's by a relative error of at most 0.0095.
Values may be sent and summed in bfloat16 or wider, within the bound.
No kernel may reach another device: no remote copies, remote signals or barrier semaphores. Data moves between devices by JAX's collectives and lax.ppermute only.
A program may use at most 64 MiB of HBM per device.

v0:
```python
import math
import jax
import jax.numpy as jnp
from jax import lax
from jax.sharding import PartitionSpec as P

CODE_BREADTH = 512
LON = 1440
MODES = 128
CAP = 2


def extended(block, sides, width):
    for axis, dim in sides:
        count = lax.axis_size(axis)
        forward = [(i, i + 1) for i in range(count - 1)]
        backward = [(target, source) for source, target in forward]
        low = lax.ppermute(
            lax.slice_in_dim(block, block.shape[dim] - width, None, axis=dim), axis, forward
        )
        high = lax.ppermute(lax.slice_in_dim(block, 0, width, axis=dim), axis, backward)
        block = jnp.concatenate([low, block, high], axis=dim)
    return block


def from_behind(value, axis, steps):
    count = lax.axis_size(axis)
    initial, last = (max(0, -steps), min(count, count - steps))
    return lax.ppermute(value, axis, [(source, source + steps) for source in range(initial, last)])


def tables():
    wavenum = jnp.arange(MODES, dtype=jnp.int32)
    lon_pos = jnp.arange(LON, dtype=jnp.int32)
    phases = (wavenum[:, None] * lon_pos[None, :] % LON).astype(jnp.float32) * (2.0 * math.pi / LON)
    forward = jnp.concatenate([jnp.cos(phases), -jnp.sin(phases)], 0).astype(jnp.bfloat16)
    weight = jnp.where(wavenum == 0, 1.0, 2.0).astype(jnp.float32) / LON
    inverse = jnp.concatenate(
        [jnp.cos(phases) * weight[:, None], -jnp.sin(phases) * weight[:, None]], 0
    ).T.astype(jnp.bfloat16)
    return (forward, inverse)


def silu_grad(values):
    logistic = jax.nn.sigmoid(values)
    return logistic * (1.0 + values * (1.0 - logistic))


def cell_table(lon_row, count_row):
    is_live = (jnp.arange(CAP, dtype=jnp.int32)[None, :] < count_row[:, None]).reshape(-1)
    matches = (lon_row[None, :] == jnp.arange(LON, dtype=jnp.int32)[:, None]) & is_live[None, :]
    return (matches.astype(jnp.bfloat16), jnp.sum(matches.astype(jnp.float32), axis=1))


def encode(rows, w_in, w_out):
    pre1 = jnp.dot(rows, w_in, preferred_element_type=jnp.float32)
    hidden = jax.nn.silu(pre1).astype(jnp.bfloat16)
    latent = jnp.dot(hidden, w_out, preferred_element_type=jnp.float32).astype(jnp.bfloat16)
    return (pre1, hidden, latent)


def encoder_grads(rows, pre1, hidden, grad_latent, w_in, w_out):
    out_local = jnp.dot(hidden.T, grad_latent, preferred_element_type=jnp.float32)
    grad_hidden = jnp.dot(grad_latent, w_out.T, preferred_element_type=jnp.float32)
    grad_pre1 = (grad_hidden * silu_grad(pre1)).astype(jnp.bfloat16)
    in_local = jnp.dot(rows.T, grad_pre1, preferred_element_type=jnp.float32)
    row_grads = jnp.dot(grad_pre1, w_in.T, preferred_element_type=jnp.float32).astype(jnp.bfloat16)
    return (in_local, out_local, row_grads)


def shards(
    observations, lon_index, live_count, w_in, w_out, w_spec, north, south, w_mix, loss_sensitivity
):
    enc_count = lax.axis_size("enc")
    blk_count = lax.axis_size("blk")
    devices = enc_count * blk_count
    slot_total = observations.shape[0]
    forward, inverse = tables()
    pre1, hidden, latent = encode(observations, w_in, w_out)
    outgoing = latent.reshape(enc_count, blk_count, CAP, CODE_BREADTH)
    arrived = lax.all_to_all(
        lax.all_to_all(outgoing, "enc", split_axis=0, concat_axis=0, tiled=True),
        "blk",
        split_axis=1,
        concat_axis=1,
        tiled=True,
    )
    lat_rows = arrived.reshape(slot_total, CODE_BREADTH)
    onehot, occupancy = cell_table(lon_index[0], live_count[0])
    denom = jnp.maximum(occupancy, 1.0)[:, None]
    grid_sum = jnp.dot(onehot, lat_rows, preferred_element_type=jnp.float32)
    resampled_field = (grid_sum / denom).astype(jnp.bfloat16)
    spectrum = jnp.dot(forward, resampled_field, preferred_element_type=jnp.float32)
    border = extended(resampled_field[None], ((("enc", "blk"), 0),), 1)
    spec_prev = jnp.dot(forward, border[0], preferred_element_type=jnp.float32)
    spec_next = jnp.dot(forward, border[2], preferred_element_type=jnp.float32)
    north_row = north[0][None, :]
    south_row = south[0][None, :]
    blended_fourier_modes = (
        spectrum * w_spec + north_row * spec_prev + south_row * spec_next
    ).astype(jnp.bfloat16)
    azimuth = jnp.dot(inverse, blended_fourier_modes, preferred_element_type=jnp.float32).astype(
        jnp.bfloat16
    )
    before_nonlinearity = jnp.dot(azimuth, w_mix, preferred_element_type=jnp.float32)
    predicted_state = (
        resampled_field.astype(jnp.float32) + jax.nn.silu(before_nonlinearity)
    ).astype(jnp.bfloat16)
    grad_pre = (loss_sensitivity[0].astype(jnp.float32) * silu_grad(before_nonlinearity)).astype(
        jnp.bfloat16
    )
    mix_local = jnp.dot(azimuth.T, grad_pre, preferred_element_type=jnp.float32)
    gridding_factor = 1.0 / math.sqrt(devices * LON)
    grad_az = jnp.dot(grad_pre, w_mix.T, preferred_element_type=jnp.float32).astype(jnp.bfloat16)
    blend_matrix_slope_local = jnp.dot(inverse.T, grad_az, preferred_element_type=jnp.float32)
    from_next = from_behind(north_row * blend_matrix_slope_local, ("enc", "blk"), -1)
    from_prev = from_behind(south_row * blend_matrix_slope_local, ("enc", "blk"), 1)
    grad_spec = (w_spec * blend_matrix_slope_local + from_next + from_prev).astype(jnp.bfloat16)
    grad_grid = loss_sensitivity[0].astype(jnp.float32) + jnp.dot(
        forward.T, grad_spec, preferred_element_type=jnp.float32
    )
    scaled = (grad_grid / denom).astype(jnp.bfloat16)
    grad_rows = jnp.dot(onehot.T, scaled, preferred_element_type=jnp.float32).astype(jnp.bfloat16)
    returned = lax.all_to_all(
        lax.all_to_all(
            grad_rows.reshape(enc_count, blk_count, CAP, CODE_BREADTH),
            "enc",
            split_axis=0,
            concat_axis=0,
            tiled=True,
        ),
        "blk",
        split_axis=1,
        concat_axis=1,
        tiled=True,
    )
    grad_latent = returned.reshape(slot_total, CODE_BREADTH)
    in_local, out_local, observation_slope = encoder_grads(
        observations, pre1, hidden, grad_latent, w_in, w_out
    )
    observed_factor = 1.0 / math.sqrt(devices * slot_total)
    input_gradient_total, output_gradient_total, blend_matrix_slope_summed = lax.psum(
        (in_local, out_local, mix_local), ("enc", "blk")
    )
    return (
        predicted_state[None],
        input_gradient_total * observed_factor,
        output_gradient_total * observed_factor,
        blend_matrix_slope_summed * gridding_factor,
        observation_slope,
    )


def solution(mesh):
    placed = (
        P(("enc", "blk"), None),
        P(("enc", "blk"), None),
        P(("enc", "blk"), None),
        P(),
        P(),
        P(),
        P(("enc", "blk"), None),
        P(("enc", "blk"), None),
        P(),
        P(("enc", "blk"), None, None),
    )
    return jax.shard_map(
        shards,
        mesh=mesh,
        in_specs=placed,
        out_specs=(P(("enc", "blk"), None, None), P(), P(), P(), P(("enc", "blk"), None)),
        check_vma=False,
    )
```

profile of v0, /device:TPU:8, one launch (start us, length us, event | category | flops | bytes accessed | tf_op | source)
XLA Modules:
  0.0 426.9 jit_solution(8997733929521939271)
XLA Ops:
  9.5 1.5 convolution_convert_fusion.2
  11.2 17.3 %all_to_all.20 = bf16[16,16,2,512]{3,2,1,0:T(2,128)(2,1)S(1)} all-to-all(bf16[16,16,2,512]{3,2,1,0:T(2,128)(2,1)S(1)} %reshape.48), channel_id=1, replica_groups=mesh['enc'=16,'blk'=16] {'enc'}, dimensions={0} | all-to-all | bytes 1048576 | tf_op jit(solution)/shard_map/all_to_all | solution.py:82
  29.8 8.6 %all-to-all-start.1 = ((bf16[16,16,2,512]{3,2,0,1:T(2,128)(2,1)}), bf16[16,16,2,512]{3,2,0,1:T(2,128)(2,1)S(1)}, u32[]{:S(2)}, u32[]{:S(2)}) async-start(bf16[16,16,2,512]{3,2,0,1:T(2,128)(2,1)} %copy.30), calls=%async_computation.1 | async-start | bytes 1048576 | tf_op jit(solution)/shard_map/all_to_all | solution.py:81
  39.2 15.2 %all-to-all-done.1 = bf16[16,16,2,512]{3,2,0,1:T(2,128)(2,1)S(1)} async-done(((bf16[16,16,2,512]{3,2,0,1:T(2,128)(2,1)}), bf16[16,16,2,512]{3,2,0,1:T(2,128)(2,1)S(1)}, u32[]{:S(2)}, u32[]{:S(2)}) %all-to-all-start.1) | async-done | bytes 524320 | tf_op jit(solution)/shard_map/all_to_all | solution.py:81
  56.1 2.9 collective-permute-start.1
  59.1 2.7 collective-permute-start
  61.8 3.5 fusion.44
  65.3 4.1 multiply_convert_fusion.2
  70.8 5.2 %collective-permute-done.1 = bf16[1,1440,512]{2,1,0:T(8,128)(2,1)S(1)} collective-permute-done((bf16[1,1440,512]{2,1,0:T(8,128)(2,1)S(1)}, bf16[1,1440,512]{2,1,0:T(8,128)(2,1)S(1)}, u32[]{:S(2)}, u32[]{:S(2)}) %collective-permute-start.1) | collective-permute-done | bytes 1474592 | tf_op jit(solution)/shard_map/ppermute | solution.py:21
  77.3 4.6 %collective-permute-done = bf16[1,1440,512]{2,1,0:T(8,128)(2,1)S(1)} collective-permute-done((bf16[1,1440,512]{2,1,0:T(8,128)(2,1)S(1)}, bf16[1,1440,512]{2,1,0:T(8,128)(2,1)S(1)}, u32[]{:S(2)}, u32[]{:S(2)}) %collective-permute-start) | collective-permute-done | bytes 1474592 | tf_op jit(solution)/shard_map/ppermute | solution.py:18
  83.0 2.9 convolution_convert_fusion.1
  85.9 5.2 %fusion = (bf16[1440,512]{1,0:T(8,128)(2,1)S(1)}, bf16[1,1440,512]{2,1,0:T(8,128)(2,1)}) fusion(bf16[1,1440,512]{2,1,0:T(8,128)(2,1)} %param.19, bf16[1440,512]{1,0:T(8,128)(2,1)} %copy-done.12, bf16[1440,512]{1,0:T(8,128)(2,1)S(1)} %convolution_convert_fusion.1, bf16[512,512]{1,0:T(8,128)(2,1)S(1)} %copy-done), kind=kOutput, calls=%fused_computation.4 | convolution fusion | flops 765296640 | bytes 7897088 | tf_op jit(solution)/shard_map/dot_general | solution.py:105
  91.1 4.2 broadcast_multiply_fusion.3
  95.3 1.9 collective-permute-start.2
  97.2 2.6 collective-permute-start.3
  99.8 4.4 %collective-permute-done.2 = f32[256,512]{1,0:T(8,128)S(1)} collective-permute-done((f32[256,512]{1,0:T(8,128)}, f32[256,512]{1,0:T(8,128)S(1)}, u32[]{:S(2)}, u32[]{:S(2)}) %collective-permute-start.2) | collective-permute-done | bytes 524320 | tf_op jit(solution)/shard_map/ppermute | solution.py:29
  104.2 5.8 %collective-permute-done.3 = f32[256,512]{1,0:T(8,128)S(1)} collective-permute-done((f32[256,512]{1,0:T(8,128)}, f32[256,512]{1,0:T(8,128)S(1)}, u32[]{:S(2)}, u32[]{:S(2)}) %collective-permute-start.3) | collective-permute-done | bytes 524320 | tf_op jit(solution)/shard_map/ppermute | solution.py:29
  110.8 3.9 fusion.17
  115.0 16.4 %all_to_all.21 = bf16[16,16,2,512]{3,2,1,0:T(2,128)(2,1)S(1)} all-to-all(bf16[16,16,2,512]{3,2,1,0:T(2,128)(2,1)S(1)} %reshape.50), channel_id=1, replica_groups=mesh['enc'=16,'blk'=16] {'enc'}, dimensions={0} | all-to-all | bytes 1048576 | tf_op jit(solution)/shard_map/all_to_all | solution.py:125
  132.6 3.6 all-to-all-start.3
  136.2 3.3 fusion.53
  139.6 12.5 %all-to-all-done.3 = bf16[16,16,2,512]{3,2,0,1:T(2,128)(2,1)S(1)} async-done(((bf16[16,16,2,512]{3,2,0,1:T(2,128)(2,1)}), bf16[16,16,2,512]{3,2,0,1:T(2,128)(2,1)S(1)}, u32[]{:S(2)}, u32[]{:S(2)}) %all-to-all-start.3) | async-done | bytes 524320 | tf_op jit(solution)/shard_map/all_to_all | solution.py:124
  152.8 2.0 fusion.20
  158.3 257.6 %all-reduce.3.cloned.1.call-done = (f32[128,512]{0,1:T(8,128)}, f32[512,512]{1,0:T(8,128)}, f32[512,512]{1,0:T(8,128)}) async-done(((f32[128,512]{0,1:T(8,128)}, f32[512,512]{1,0:T(8,128)}, f32[512,512]{1,0:T(8,128)}), (f32[128,512]{0,1:T(8,128)}, f32[512,512]{1,0:T(8,128)}, f32[512,512]{1,0:T(8,128)})) %all-reduce.3.cloned.1.call-update) | async-done | bytes 2359312 | tf_op jit(solution)/shard_map/psum | solution.py:142
  (66 shorter events, 20.9 us)
Async XLA Ops:
  7.2 78.7 %copy-start = (bf16[512,512]{1,0:T(8,128)(2,1)S(1)}, bf16[512,512]{1,0:T(8,128)(2,1)}, u32[]{:S(2)}) copy-start(bf16[512,512]{1,0:T(8,128)(2,1)} %param.18) | copy-start | bytes 1572868
  11.2 27.2 %copy-start.11 = (s32[1,256]{1,0:T(1,128)S(1)}, s32[1,256]{1,0:T(1,128)}, u32[]{:S(2)}) copy-start(s32[1,256]{1,0:T(1,128)} %param.12) | copy-start | bytes 3076
  11.2 27.5 %copy-start.19 = (s32[1,512]{1,0:T(1,128)S(1)}, s32[1,512]{1,0:T(1,128)}, u32[]{:S(2)}) copy-start(s32[1,512]{1,0:T(1,128)} %param.11) | copy-start | bytes 6148
  29.8 24.6 %all-to-all-start.1 = ((bf16[16,16,2,512]{3,2,0,1:T(2,128)(2,1)}), bf16[16,16,2,512]{3,2,0,1:T(2,128)(2,1)S(1)}, u32[]{:S(2)}, u32[]{:S(2)}) async-start(bf16[16,16,2,512]{3,2,0,1:T(2,128)(2,1)} %copy.30), calls=%async_computation.1 | async-start | bytes 1048576 | tf_op jit(solution)/shard_map/all_to_all | solution.py:81
  56.1 14.7 %copy-start.12 = (bf16[1440,512]{1,0:T(8,128)(2,1)}, bf16[1440,512]{1,0:T(8,128)(2,1)S(1)}, u32[]{:S(2)}) copy-start(bf16[1440,512]{1,0:T(8,128)(2,1)S(1)} %divide_convert_fusion.1) | copy-start | bytes 4423684
  56.1 13.3 %copy-start.14 = (f32[256,512]{1,0:T(8,128)S(1)}, f32[256,512]{1,0:T(8,128)}, u32[]{:S(2)}) copy-start(f32[256,512]{1,0:T(8,128)} %param.15) | copy-start | bytes 1572868
  56.1 19.8 %collective-permute-start.1 = (bf16[1,1440,512]{2,1,0:T(8,128)(2,1)S(1)}, bf16[1,1440,512]{2,1,0:T(8,128)(2,1)S(1)}, u32[]{:S(2)}, u32[]{:S(2)}) collective-permute-start(bf16[1,1440,512]{2,1,0:T(8,128)(2,1)S(1)} %bitcast.52), channel_id=1, source_target_pairs={{1,0},{2,1},{3,2},{4,3},{5,4},{6,5},{7,6},{8,7},{9,8},{10,9},{11,1... | collective-permute-start | bytes 4423688 | tf_op jit(solution)/shard_map/ppermute | solution.py:21
  59.1 22.8 %collective-permute-start = (bf16[1,1440,512]{2,1,0:T(8,128)(2,1)S(1)}, bf16[1,1440,512]{2,1,0:T(8,128)(2,1)S(1)}, u32[]{:S(2)}, u32[]{:S(2)}) collective-permute-start(bf16[1,1440,512]{2,1,0:T(8,128)(2,1)S(1)} %bitcast.53), channel_id=1, source_target_pairs={{0,1},{1,2},{2,3},{3,4},{4,5},{5,6},{6,7},{7,8},{8,9},{9,10},{10,1... | collective-permute-start | bytes 4423688 | tf_op jit(solution)/shard_map/ppermute | solution.py:18
  65.3 17.7 %copy-start.8 = (bf16[128,1440]{1,0:T(8,128)(2,1)}, bf16[128,1440]{1,0:T(8,128)(2,1)S(1)}, u32[]{:S(2)}) copy-start(bf16[128,1440]{1,0:T(8,128)(2,1)S(1)} %get-tuple-element.45) | copy-start | bytes 1105924
  65.3 17.7 %copy-start.9 = (bf16[128,1440]{1,0:T(8,128)(2,1)}, bf16[128,1440]{1,0:T(8,128)(2,1)S(1)}, u32[]{:S(2)}) copy-start(bf16[128,1440]{1,0:T(8,128)(2,1)S(1)} %get-tuple-element.46) | copy-start | bytes 1105924
  69.4 13.6 %copy-start.10 = (bf16[128,1440]{1,0:T(8,128)(2,1)}, bf16[128,1440]{1,0:T(8,128)(2,1)S(1)}, u32[]{:S(2)}) copy-start(bf16[128,1440]{1,0:T(8,128)(2,1)S(1)} %get-tuple-element.42) | copy-start | bytes 1105924
  69.4 6.5 %copy-start.17 = (f32[1,512]{1,0:T(1,128)S(1)}, f32[1,512]{1,0:T(1,128)}, u32[]{:S(2)}) copy-start(f32[1,512]{1,0:T(1,128)} %param.17) | copy-start | bytes 6148
  76.0 7.1 %copy-start.18 = (f32[1,512]{1,0:T(1,128)S(1)}, f32[1,512]{1,0:T(1,128)}, u32[]{:S(2)}) copy-start(f32[1,512]{1,0:T(1,128)} %param.16) | copy-start | bytes 6148
  81.9 1.1 copy-start.13
  91.1 4.2 copy-start.1
  95.3 8.9 %collective-permute-start.2 = (f32[256,512]{1,0:T(8,128)}, f32[256,512]{1,0:T(8,128)S(1)}, u32[]{:S(2)}, u32[]{:S(2)}) collective-permute-start(f32[256,512]{1,0:T(8,128)} %get-tuple-element.40), channel_id=1, source_target_pairs={{1,0},{2,1},{3,2},{4,3},{5,4},{6,5},{7,6},{8,7},{9,8},{10,9},{11,1... | collective-permute-start | bytes 1572872 | tf_op jit(solution)/shard_map/ppermute | solution.py:29
  97.2 12.8 %collective-permute-start.3 = (f32[256,512]{1,0:T(8,128)}, f32[256,512]{1,0:T(8,128)S(1)}, u32[]{:S(2)}, u32[]{:S(2)}) collective-permute-start(f32[256,512]{1,0:T(8,128)} %get-tuple-element.41), channel_id=1, source_target_pairs={{0,1},{1,2},{2,3},{3,4},{4,5},{5,6},{6,7},{7,8},{8,9},{9,10},{10,1... | collective-permute-start | bytes 1572872 | tf_op jit(solution)/shard_map/ppermute | solution.py:29
  132.6 19.5 %all-to-all-start.3 = ((bf16[16,16,2,512]{3,2,0,1:T(2,128)(2,1)}), bf16[16,16,2,512]{3,2,0,1:T(2,128)(2,1)S(1)}, u32[]{:S(2)}, u32[]{:S(2)}) async-start(bf16[16,16,2,512]{3,2,0,1:T(2,128)(2,1)} %copy.32), calls=%async_computation.3 | async-start | bytes 1048576 | tf_op jit(solution)/shard_map/all_to_all | solution.py:124
  136.2 279.7 %all-reduce.3.cloned.1.call-start = ((), (), s32[]{:S(2)}) async-start(), calls=%async_computation.4 | async-start | bytes 4718592 | tf_op jit(solution)/shard_map/psum | solution.py:142
  139.6 13.2 %copy-start.15 = (bf16[512,512]{1,0:T(8,128)(2,1)S(1)}, bf16[512,512]{1,0:T(8,128)(2,1)}, u32[]{:S(2)}) copy-start(bf16[512,512]{1,0:T(8,128)(2,1)} %param.14) | copy-start | bytes 1572868
  152.8 2.0 copy-start.3
  154.8 1.5 copy-start.6
  415.9 2.0 copy-start.5
  415.9 3.1 copy-start.4
  (3 other events, 2.8 us)
Sparse Core Ops, SparseCore 0:
  157.5 258.3 all-reduce.2
where the time goes:
time: 428 us; the launch traced here: 427 us
  waiting for transfers between devices  305 us (71%)
  blocking collectives  33.7 us (8%)
  matrix products  31.5 us (7%)
  starting transfers between devices  22.3 us (5%)
  between operations  14.3 us (3%)
  other arithmetic  11.5 us (3%)
  local copies, waits for them, and re-layouts  8.33 us (2%)
    psum x1, waiting for transfers between devices, shards(): lax.psum((in_local, out_local, mix_local), ('enc', 'blk'))  258 us
    all_to_all x1, blocking collectives, shards(): lax.all_to_all(outgoing, 'enc', split_axis=0, concat_axis=0, tiled=True)  17.3 us
    all_to_all x1, blocking collectives, shards(): lax.all_to_all(grad_rows.reshape(enc_count, blk_count, CAP, CODE_BREADTH)...  16.4 us
    all_to_all x1, waiting for transfers between devices, shards(): lax.all_to_all(lax.all_to_all(outgoing, 'enc', split_axis=0, concat_axis=...  15.2 us
    all_to_all x1, waiting for transfers between devices, shards(): lax.all_to_all(lax.all_to_all(grad_rows.reshape(enc_count, blk_count, CAP...  12.5 us
    ppermute x2, waiting for transfers between devices, from_behind(): lax.ppermute(value, axis, [(source, source + steps) for source in range(i...  10.2 us
    all_to_all x1, starting transfers between devices, shards(): lax.all_to_all(lax.all_to_all(outgoing, 'enc', split_axis=0, concat_axis=...  8.58 us
  transfers between devices with their start and end apart: 7, of which 7 were waited for; matrix products, arithmetic and copies ran while one was open for 4% of the time, Pallas kernels for 0%

commit v1 on v0

--- a/solution.py
+++ b/solution.py
@@ -140,7 +140,7 @@
     )
     observed_factor = 1.0 / math.sqrt(devices * slot_total)
     input_gradient_total, output_gradient_total, blend_matrix_slope_summed = lax.psum(
-        (in_local, out_local, mix_local), ("enc", "blk")
+        lax.psum((in_local, out_local, mix_local), "blk"), "enc"
     )
     return (
         predicted_state[None],

time: 428 us -> 388 us (0.907)
  waiting for transfers between devices: 305 us -> 264 us
    psum x1 -> x2, waiting for transfers between devices: 258 us -> 217 us  [the longest x1 112 us: shards(): lax.psum((in_local, out_local, mix_local), 'blk')]
  transfers between devices with their start and end apart: 7 -> 8, of which waited for: 7 -> 8; matrix products, arithmetic and copies ran while one was open for 4% -> 4% of each run, Pallas kernels for 0% -> 0%
where the time goes in v1:
time: 388 us; the launch traced here: 386 us
  waiting for transfers between devices  264 us (68%)
  blocking collectives  33.7 us (9%)
  matrix products  31.5 us (8%)
  starting transfers between devices  22.4 us (6%)
  between operations  14.4 us (4%)
  other arithmetic  11.5 us (3%)
  local copies, waits for them, and re-layouts  8.33 us (2%)
    psum x1, waiting for transfers between devices, shards(): lax.psum((in_local, out_local, mix_local), 'blk')  112 us
    psum x1, waiting for transfers between devices, shards(): lax.psum(lax.psum((in_local, out_local, mix_local), 'blk'), 'enc')  104 us
    all_to_all x1, blocking collectives, shards(): lax.all_to_all(outgoing, 'enc', split_axis=0, concat_axis=0, tiled=True)  17.3 us
    all_to_all x1, blocking collectives, shards(): lax.all_to_all(grad_rows.reshape(enc_count, blk_count, CAP, CODE_BREADTH)...  16.4 us
    all_to_all x1, waiting for transfers between devices, shards(): lax.all_to_all(lax.all_to_all(outgoing, 'enc', split_axis=0, concat_axis=...  15.2 us
    all_to_all x1, waiting for transfers between devices, shards(): lax.all_to_all(lax.all_to_all(grad_rows.reshape(enc_count, blk_count, CAP...  12.5 us
    ppermute x2, waiting for transfers between devices, from_behind(): lax.ppermute(value, axis, [(source, source + steps) for source in range(i...  10.2 us
    all_to_all x1, starting transfers between devices, shards(): lax.all_to_all(lax.all_to_all(outgoing, 'enc', split_axis=0, concat_axis=...  8.58 us
  transfers between devices with their start and end apart: 8, of which 8 were waited for; matrix products, arithmetic and copies ran while one was open for 4% of the time, Pallas kernels for 0%

profile of v1, /device:TPU:8, one launch (start us, length us, event | category | flops | bytes accessed | tf_op | source)
XLA Modules:
  0.0 386.1 jit_solution(11060997996489895265)
XLA Ops:
  11.2 17.3 %all_to_all.20 = bf16[16,16,2,512]{3,2,1,0:T(2,128)(2,1)S(1)} all-to-all(bf16[16,16,2,512]{3,2,1,0:T(2,128)(2,1)S(1)} %reshape.48), channel_id=1, replica_groups=mesh['enc'=16,'blk'=16] {'enc'}, dimensions={0} | all-to-all | bytes 1048576 | tf_op jit(solution)/shard_map/all_to_all | solution.py:82
  29.8 8.6 %all-to-all-start.1 = ((bf16[16,16,2,512]{3,2,0,1:T(2,128)(2,1)}), bf16[16,16,2,512]{3,2,0,1:T(2,128)(2,1)S(1)}, u32[]{:S(2)}, u32[]{:S(2)}) async-start(bf16[16,16,2,512]{3,2,0,1:T(2,128)(2,1)} %copy.30), calls=%async_computation.1 | async-start | bytes 1048576 | tf_op jit(solution)/shard_map/all_to_all | solution.py:81
  39.2 15.2 %all-to-all-done.1 = bf16[16,16,2,512]{3,2,0,1:T(2,128)(2,1)S(1)} async-done(((bf16[16,16,2,512]{3,2,0,1:T(2,128)(2,1)}), bf16[16,16,2,512]{3,2,0,1:T(2,128)(2,1)S(1)}, u32[]{:S(2)}, u32[]{:S(2)}) %all-to-all-start.1) | async-done | bytes 524320 | tf_op jit(solution)/shard_map/all_to_all | solution.py:81
  56.1 2.9 collective-permute-start.1
  59.1 2.7 collective-permute-start
  61.8 3.5 fusion.44
  65.3 4.1 %multiply_convert_fusion.2 = (bf16[128,1440]{1,0:T(8,128)(2,1)S(1)}, bf16[128,1440]{1,0:T(8,128)(2,1)}) fusion(f32[128]{0:T(128)S(1)} %fusion.48), kind=kLoop, calls=%fused_computation.45 | loop fusion | flops 2580480 | bytes 737792 | tf_op jit(solution)/shard_map/convert.3
  70.8 5.1 %collective-permute-done.1 = bf16[1,1440,512]{2,1,0:T(8,128)(2,1)S(1)} collective-permute-done((bf16[1,1440,512]{2,1,0:T(8,128)(2,1)S(1)}, bf16[1,1440,512]{2,1,0:T(8,128)(2,1)S(1)}, u32[]{:S(2)}, u32[]{:S(2)}) %collective-permute-start.1) | collective-permute-done | bytes 1474592 | tf_op jit(solution)/shard_map/ppermute | solution.py:21
  77.3 4.6 %collective-permute-done = bf16[1,1440,512]{2,1,0:T(8,128)(2,1)S(1)} collective-permute-done((bf16[1,1440,512]{2,1,0:T(8,128)(2,1)S(1)}, bf16[1,1440,512]{2,1,0:T(8,128)(2,1)S(1)}, u32[]{:S(2)}, u32[]{:S(2)}) %collective-permute-start) | collective-permute-done | bytes 1474592 | tf_op jit(solution)/shard_map/ppermute | solution.py:18
  83.1 2.9 convolution_convert_fusion.1
  85.9 5.2 %fusion = (bf16[1440,512]{1,0:T(8,128)(2,1)S(1)}, bf16[1,1440,512]{2,1,0:T(8,128)(2,1)}) fusion(bf16[1,1440,512]{2,1,0:T(8,128)(2,1)} %param.19, bf16[1440,512]{1,0:T(8,128)(2,1)} %copy-done.12, bf16[1440,512]{1,0:T(8,128)(2,1)S(1)} %convolution_convert_fusion.1, bf16[512,512]{1,0:T(8,128)(2,1)S(1)} %copy-done), kind=kOutput, calls=%fused_computation.4 | convolution fusion | flops 765296640 | bytes 7897088 | tf_op jit(solution)/shard_map/dot_general | solution.py:105
  91.1 4.2 %broadcast_multiply_fusion.3 = (f32[256,512]{1,0:T(8,128)}, f32[256,512]{1,0:T(8,128)}, f32[256,512]{1,0:T(8,128)}) fusion(f32[512]{0:T(512)S(1)} %bitcast.57, f32[512]{0:T(512)S(1)} %bitcast.55, bf16[1440,512]{1,0:T(8,128)(2,1)S(1)} %get-tuple-element.41, bf16[512,512]{1,0:T(8,128)(2,1)S(1)} %copy-done, bf16[128,1440]{1,0:T(8,128)(2,1)} %get-tuple-element.46, ...), kind=kOutput, calls=%fused_computation.57 | convolution fusion | flops 1134936064 | bytes 4313088 | tf_op jit(solution)/shard_map/dot_general | solution.py:115
  95.3 1.9 collective-permute-start.2
  97.2 2.6 collective-permute-start.3
  99.8 4.4 %collective-permute-done.2 = f32[256,512]{1,0:T(8,128)S(1)} collective-permute-done((f32[256,512]{1,0:T(8,128)}, f32[256,512]{1,0:T(8,128)S(1)}, u32[]{:S(2)}, u32[]{:S(2)}) %collective-permute-start.2) | collective-permute-done | bytes 524320 | tf_op jit(solution)/shard_map/ppermute | solution.py:29
  104.2 5.8 %collective-permute-done.3 = f32[256,512]{1,0:T(8,128)S(1)} collective-permute-done((f32[256,512]{1,0:T(8,128)}, f32[256,512]{1,0:T(8,128)S(1)}, u32[]{:S(2)}, u32[]{:S(2)}) %collective-permute-start.3) | collective-permute-done | bytes 524320 | tf_op jit(solution)/shard_map/ppermute | solution.py:29
  110.9 3.9 %fusion.17 = bf16[512,512]{1,0:T(8,128)(2,1)S(1)} fusion(s32[512]{0:T(512)S(1)} %bitcast.60, pred[512]{0:T(512)(128)(4,1)S(1)} %lt.38, bf16[1,1440,512]{2,1,0:T(8,128)(2,1)} %param.19, f32[1440]{0:T(1024)S(1)} %broadcast_maximum_fusion, f32[256,512]{1,0:T(8,128)} %copy-done.16, f32[256,512]{1,0:T(8,128)S(1)} %collective-permute-done.2, ...), kind=kOutput, calls=%fused_computation.24 | convolution fusion | flops 1139146752 | bytes 4841600 | tf_op jit(solution)/shard_map/dot_general | solution.py:123
  115.0 16.4 %all_to_all.21 = bf16[16,16,2,512]{3,2,1,0:T(2,128)(2,1)S(1)} all-to-all(bf16[16,16,2,512]{3,2,1,0:T(2,128)(2,1)S(1)} %reshape.50), channel_id=1, replica_groups=mesh['enc'=16,'blk'=16] {'enc'}, dimensions={0} | all-to-all | bytes 1048576 | tf_op jit(solution)/shard_map/all_to_all | solution.py:125
  132.6 3.6 all-to-all-start.3
  136.2 3.4 fusion.53
  139.6 12.5 %all-to-all-done.3 = bf16[16,16,2,512]{3,2,0,1:T(2,128)(2,1)S(1)} async-done(((bf16[16,16,2,512]{3,2,0,1:T(2,128)(2,1)}), bf16[16,16,2,512]{3,2,0,1:T(2,128)(2,1)S(1)}, u32[]{:S(2)}, u32[]{:S(2)}) %all-to-all-start.3) | async-done | bytes 524320 | tf_op jit(solution)/shard_map/all_to_all | solution.py:124
  152.8 2.0 fusion.20
  157.4 112.3 %all-reduce.5.cloned.1.call-done = (f32[128,512]{0,1:T(8,128)}, f32[512,512]{1,0:T(8,128)}, f32[512,512]{1,0:T(8,128)}) async-done(((f32[128,512]{0,1:T(8,128)}, f32[512,512]{1,0:T(8,128)}, f32[512,512]{1,0:T(8,128)}), (f32[128,512]{0,1:T(8,128)}, f32[512,512]{1,0:T(8,128)}, f32[512,512]{1,0:T(8,128)})) %all-reduce.5.cloned.1.call-update) | async-done | bytes 2359312 | tf_op jit(solution)/shard_map/psum | solution.py:143
  270.7 104.4 %all-reduce.7.cloned.1.call-done = (f32[128,512]{0,1:T(8,128)}, f32[512,512]{1,0:T(8,128)}, f32[512,512]{1,0:T(8,128)}) async-done(((f32[128,512]{0,1:T(8,128)}, f32[512,512]{1,0:T(8,128)}, f32[512,512]{1,0:T(8,128)}), (f32[128,512]{0,1:T(8,128)}, f32[512,512]{1,0:T(8,128)}, f32[512,512]{1,0:T(8,128)})) %all-reduce.7.cloned.1.call-update) | async-done | bytes 2359312 | tf_op jit(solution)/shard_map/psum | solution.py:142
  (69 shorter events, 22.4 us)
Async XLA Ops:
  7.2 78.7 %copy-start = (bf16[512,512]{1,0:T(8,128)(2,1)S(1)}, bf16[512,512]{1,0:T(8,128)(2,1)}, u32[]{:S(2)}) copy-start(bf16[512,512]{1,0:T(8,128)(2,1)} %param.18) | copy-start | bytes 1572868
  11.2 27.2 %copy-start.11 = (s32[1,256]{1,0:T(1,128)S(1)}, s32[1,256]{1,0:T(1,128)}, u32[]{:S(2)}) copy-start(s32[1,256]{1,0:T(1,128)} %param.12) | copy-start | bytes 3076
  11.2 27.5 %copy-start.19 = (s32[1,512]{1,0:T(1,128)S(1)}, s32[1,512]{1,0:T(1,128)}, u32[]{:S(2)}) copy-start(s32[1,512]{1,0:T(1,128)} %param.11) | copy-start | bytes 6148
  29.8 24.6 %all-to-all-start.1 = ((bf16[16,16,2,512]{3,2,0,1:T(2,128)(2,1)}), bf16[16,16,2,512]{3,2,0,1:T(2,128)(2,1)S(1)}, u32[]{:S(2)}, u32[]{:S(2)}) async-start(bf16[16,16,2,512]{3,2,0,1:T(2,128)(2,1)} %copy.30), calls=%async_computation.1 | async-start | bytes 1048576 | tf_op jit(solution)/shard_map/all_to_all | solution.py:81
  56.1 14.7 %copy-start.12 = (bf16[1440,512]{1,0:T(8,128)(2,1)}, bf16[1440,512]{1,0:T(8,128)(2,1)S(1)}, u32[]{:S(2)}) copy-start(bf16[1440,512]{1,0:T(8,128)(2,1)S(1)} %divide_convert_fusion.1) | copy-start | bytes 4423684
  56.1 13.3 %copy-start.14 = (f32[256,512]{1,0:T(8,128)S(1)}, f32[256,512]{1,0:T(8,128)}, u32[]{:S(2)}) copy-start(f32[256,512]{1,0:T(8,128)} %param.15) | copy-start | bytes 1572868
  56.1 19.8 %collective-permute-start.1 = (bf16[1,1440,512]{2,1,0:T(8,128)(2,1)S(1)}, bf16[1,1440,512]{2,1,0:T(8,128)(2,1)S(1)}, u32[]{:S(2)}, u32[]{:S(2)}) collective-permute-start(bf16[1,1440,512]{2,1,0:T(8,128)(2,1)S(1)} %bitcast.52), channel_id=1, source_target_pairs={{1,0},{2,1},{3,2},{4,3},{5,4},{6,5},{7,6},{8,7},{9,8},{10,9},{11,1... | collective-permute-start | bytes 4423688 | tf_op jit(solution)/shard_map/ppermute | solution.py:21
  59.1 22.8 %collective-permute-start = (bf16[1,1440,512]{2,1,0:T(8,128)(2,1)S(1)}, bf16[1,1440,512]{2,1,0:T(8,128)(2,1)S(1)}, u32[]{:S(2)}, u32[]{:S(2)}) collective-permute-start(bf16[1,1440,512]{2,1,0:T(8,128)(2,1)S(1)} %bitcast.53), channel_id=1, source_target_pairs={{0,1},{1,2},{2,3},{3,4},{4,5},{5,6},{6,7},{7,8},{8,9},{9,10},{10,1... | collective-permute-start | bytes 4423688 | tf_op jit(solution)/shard_map/ppermute | solution.py:18
  65.3 17.7 %copy-start.8 = (bf16[128,1440]{1,0:T(8,128)(2,1)}, bf16[128,1440]{1,0:T(8,128)(2,1)S(1)}, u32[]{:S(2)}) copy-start(bf16[128,1440]{1,0:T(8,128)(2,1)S(1)} %get-tuple-element.48) | copy-start | bytes 1105924
  65.3 17.7 %copy-start.9 = (bf16[128,1440]{1,0:T(8,128)(2,1)}, bf16[128,1440]{1,0:T(8,128)(2,1)S(1)}, u32[]{:S(2)}) copy-start(bf16[128,1440]{1,0:T(8,128)(2,1)S(1)} %get-tuple-element.49) | copy-start | bytes 1105924
  69.4 13.6 %copy-start.10 = (bf16[128,1440]{1,0:T(8,128)(2,1)}, bf16[128,1440]{1,0:T(8,128)(2,1)S(1)}, u32[]{:S(2)}) copy-start(bf16[128,1440]{1,0:T(8,128)(2,1)S(1)} %get-tuple-element.45) | copy-start | bytes 1105924
  69.4 6.5 %copy-start.17 = (f32[1,512]{1,0:T(1,128)S(1)}, f32[1,512]{1,0:T(1,128)}, u32[]{:S(2)}) copy-start(f32[1,512]{1,0:T(1,128)} %param.17) | copy-start | bytes 6148
  76.0 7.1 %copy-start.18 = (f32[1,512]{1,0:T(1,128)S(1)}, f32[1,512]{1,0:T(1,128)}, u32[]{:S(2)}) copy-start(f32[1,512]{1,0:T(1,128)} %param.16) | copy-start | bytes 6148
  91.1 4.2 %copy-start.1 = (bf16[1440,512]{1,0:T(8,128)(2,1)}, bf16[1440,512]{1,0:T(8,128)(2,1)S(1)}, u32[]{:S(2)}) copy-start(bf16[1440,512]{1,0:T(8,128)(2,1)S(1)} %get-tuple-element.41) | copy-start | bytes 4423684
  95.3 8.9 %collective-permute-start.2 = (f32[256,512]{1,0:T(8,128)}, f32[256,512]{1,0:T(8,128)S(1)}, u32[]{:S(2)}, u32[]{:S(2)}) collective-permute-start(f32[256,512]{1,0:T(8,128)} %get-tuple-element.43), channel_id=1, source_target_pairs={{1,0},{2,1},{3,2},{4,3},{5,4},{6,5},{7,6},{8,7},{9,8},{10,9},{11,1... | collective-permute-start | bytes 1572872 | tf_op jit(solution)/shard_map/ppermute | solution.py:29
  97.2 12.8 %collective-permute-start.3 = (f32[256,512]{1,0:T(8,128)}, f32[256,512]{1,0:T(8,128)S(1)}, u32[]{:S(2)}, u32[]{:S(2)}) collective-permute-start(f32[256,512]{1,0:T(8,128)} %get-tuple-element.44), channel_id=1, source_target_pairs={{0,1},{1,2},{2,3},{3,4},{4,5},{5,6},{6,7},{7,8},{8,9},{9,10},{10,1... | collective-permute-start | bytes 1572872 | tf_op jit(solution)/shard_map/ppermute | solution.py:29
  132.6 19.5 %all-to-all-start.3 = ((bf16[16,16,2,512]{3,2,0,1:T(2,128)(2,1)}), bf16[16,16,2,512]{3,2,0,1:T(2,128)(2,1)S(1)}, u32[]{:S(2)}, u32[]{:S(2)}) async-start(bf16[16,16,2,512]{3,2,0,1:T(2,128)(2,1)} %copy.32), calls=%async_computation.3 | async-start | bytes 1048576 | tf_op jit(solution)/shard_map/all_to_all | solution.py:124
  136.2 133.5 %all-reduce.5.cloned.1.call-start = ((), (), s32[]{:S(2)}) async-start(), calls=%async_computation.4 | async-start | bytes 4718592 | tf_op jit(solution)/shard_map/psum | solution.py:143
  139.6 13.2 %copy-start.15 = (bf16[512,512]{1,0:T(8,128)(2,1)S(1)}, bf16[512,512]{1,0:T(8,128)(2,1)}, u32[]{:S(2)}) copy-start(bf16[512,512]{1,0:T(8,128)(2,1)} %param.14) | copy-start | bytes 1572868
  152.8 2.0 copy-start.3
  157.4 112.4 %copy-start.7 = (bf16[128,512]{1,0:T(8,128)(2,1)S(1)}, bf16[128,512]{1,0:T(8,128)(2,1)}, u32[]{:S(2)}) copy-start(bf16[128,512]{1,0:T(8,128)(2,1)} %param.13) | copy-start | bytes 393220
  157.4 217.7 %all-reduce.7.cloned.1.call-start = ((), (), s32[]{:S(2)}) async-start(), calls=%async_computation.5 | async-start | bytes 4718592 | tf_op jit(solution)/shard_map/psum | solution.py:142
  375.1 2.0 copy-start.5
  375.1 3.1 copy-start.4
  (4 other events, 4.4 us)
Sparse Core Ops, SparseCore 0:
  157.5 112.1 all-reduce.4
  273.3 101.7 all-reduce.6
